TPU v7x, 512 devices: a whole 4x4x16 slice. The times are simulated.
512 devices in a mesh: ctx: 32 (over x_lo, z), fsdp: 16 (over x_hi, y, core).
Axes of the slice: x: 4 (x_hi: 2, x_lo: 2; x = x_hi * 2 + x_lo), y: 4, z: 16, core: 2. Of those that a mesh axis runs over, the one named last changes fastest.
Arguments:
- streams: bfloat16 [16, 4096, 12288], P('fsdp', 'ctx'), may hold values from -18 to 18
- filters: float32 [3, 3, 4096], P(None, None, 'fsdp'), may hold values from 0.1 to 1.9
Outputs:
- attended: bfloat16 [16, 4096, 4096], P('fsdp', 'ctx')
All inputs are finite; a program needn't handle non-finite values.
Results may differ from a plain program's by a relative error of at most 0.011.
Values may be sent and summed in bfloat16 or wider, within the bound.
No kernel may reach another device: no remote copies, remote signals or barrier semaphores. Data moves between devices by JAX's collectives and lax.ppermute only.
A program may use at most 64 MiB of HBM per device.

v0:
```python
import jax
import jax.numpy as jnp
from jax import lax
from jax.sharding import PartitionSpec as P

HEADS = 32
HEAD_DIM = 128
TAPS = 3


def passed_along(value, axis, steps):
    count = lax.axis_size(axis)
    first, last = (max(0, -steps), min(count, count - steps))
    return lax.ppermute(value, axis, [(source, source + steps) for source in range(first, last)])


def for_sending(array):

    def short(part):
        return part.astype(jnp.bfloat16) if part.dtype == jnp.float32 else part

    return jax.tree.map(short, array)


def featurize(grouped, left_rim, tap_table):
    count = grouped.shape[1]
    extended = jnp.concatenate([left_rim, grouped], axis=1)
    summed = jnp.zeros(grouped.shape, jnp.float32)
    for offset in range(TAPS):
        window = extended[:, TAPS - 1 - offset : TAPS - 1 - offset + count]
        summed = summed + tap_table[:, offset] * window.astype(jnp.float32)
    return summed.astype(jnp.bfloat16)


def attend_one(sequence):
    length_all = sequence.shape[0]
    block_rows = max(512, length_all // 8)
    queries = sequence[:, 0]
    keys_all = sequence[:, 1]
    values_all = sequence[:, 2]
    scale_factor = sequence.shape[-1] ** (-0.5)
    pieces = []
    for number in range(length_all // block_rows):
        first = number * block_rows
        final = first + block_rows
        scores = (
            jnp.einsum(
                "qhe,khe->hqk",
                queries[first:final],
                keys_all[:final],
                preferred_element_type=jnp.float32,
            )
            * scale_factor
        )
        query_pos = first + jnp.arange(block_rows)
        key_pos = jnp.arange(final)
        scores = jnp.where(key_pos[None, None, :] <= query_pos[None, :, None], scores, -jnp.inf)
        highest = jnp.max(scores, axis=-1, keepdims=True)
        exponent = jnp.exp(scores - highest)
        totals = jnp.sum(exponent, axis=-1)
        weights = exponent.astype(jnp.bfloat16)
        summed = jnp.einsum(
            "hqk,khe->qhe", weights, values_all[:final], preferred_element_type=jnp.float32
        )
        pieces.append((summed / totals.T[:, :, None]).astype(jnp.bfloat16))
    return jnp.concatenate(pieces, axis=0)


def on_device(streams, filters):
    seqs_here, positions, channel_width = streams.shape
    tap_table = lax.all_gather(filters, "fsdp", axis=2, tiled=True).reshape(
        3, TAPS, HEADS, HEAD_DIM
    )
    grouped = streams.reshape(seqs_here, positions, 3, HEADS, HEAD_DIM)
    left_rim = passed_along(grouped[:, positions - (TAPS - 1) :], "ctx", 1)
    outgoing = featurize(grouped, left_rim, tap_table)
    per_head = lax.map(
        attend_one, lax.all_to_all(outgoing, "ctx", split_axis=3, concat_axis=1, tiled=True)
    )
    returned = lax.all_to_all(
        for_sending(per_head), "ctx", split_axis=1, concat_axis=2, tiled=True
    ).astype(per_head.dtype)
    return returned.reshape(seqs_here, positions, HEADS * HEAD_DIM)


def solution(mesh):
    placed = (P("fsdp", "ctx", None), P(None, None, "fsdp"))
    return jax.shard_map(
        on_device, mesh=mesh, in_specs=placed, out_specs=P("fsdp", "ctx", None), check_vma=False
    )
```

profile of v0, /device:TPU:32, one launch (start us, length us, event | category | flops | bytes accessed | tf_op | source)
XLA Modules:
  0.0 331.6 jit_solution(4726981693076884133)
XLA Ops:
  0.0 3.5 %copy.34 = bf16[1,128,12288]{1,2,0:T(8,128)(2,1)S(1)} copy(bf16[1,128,12288]{2,1,0:T(8,128)(2,1)} %param.2) | data formatting | bytes 6291456 | tf_op args[0]
  3.5 2.6 slice.192
  6.1 3.2 copy.36
  9.3 3.8 %collective-permute-start = (bf16[1,2,3,32,128]{4,3,2,1,0:T(8,128)(2,1)S(1)}, bf16[1,2,3,32,128]{4,3,2,1,0:T(8,128)(2,1)}, u32[]{:S(2)}, u32[]{:S(2)}) collective-permute-start(bf16[1,2,3,32,128]{4,3,2,1,0:T(8,128)(2,1)S(1)} %copy.36), channel_id=1, source_target_pairs={{0,16},{16,32},{32,48},{48,64},{64,80},{80,96},{96,112},{112,128},... | collective-permute-start | bytes 147464 | tf_op jit(solution)/shard_map/ppermute | solution.py:14
  13.2 24.9 %all_gather.3 = f32[3,3,4096]{2,1,0:T(4,128)S(1)} all-gather(f32[3,3,256]{2,1,0:T(4,128)S(1)} %copy-done.1), channel_id=1, replica_groups=mesh['ctx'=32,'fsdp'=16] {'fsdp'}, dimensions={2}, use_global_device_ids=true | all-gather | bytes 156672 | tf_op jit(solution)/shard_map/all_gather | solution.py:71
  38.3 3.5 %copy.37 = bf16[1,2,3,32,128]{1,4,3,2,0:T(8,128)(2,1)} copy(bf16[1,2,3,32,128]{4,3,2,1,0:T(8,128)(2,1)} %collective-permute-done) | data formatting | bytes 98304 | tf_op jit(solution)/shard_map/ppermute | solution.py:14
  41.8 10.0 %add_convert_fusion = bf16[1,128,3,32,128]{1,4,3,2,0:T(8,128)(2,1)S(1)} fusion(bf16[1,128,3,32,128]{1,4,3,2,0:T(8,128)(2,1)S(1)} %bitcast.242, bf16[1,2,3,32,128]{1,4,3,2,0:T(8,128)(2,1)} %copy.37, f32[3,32,128]{2,1,0:T(8,128)S(1)} %get-tuple-element.16, f32[3,32,128]{2,1,0:T(8,128)S(1)} %get-tuple-element.14, f32[3,32,128]{2,1,0:T(8,128)S(1)} %get-tuple-element.12), kind=kLoop, calls=%fused_computation.15 | loop fusion | flops 23592960 | bytes 6488064 | tf_op jit(solution)/shard_map/convert_element_type | solution.py:32
  51.9 2.1 copy.39
  54.0 14.5 %all-to-all-start = ((bf16[1,128,3,32,128]{1,4,2,0,3:T(8,128)(2,1)}), bf16[1,128,3,32,128]{1,4,2,0,3:T(8,128)(2,1)}, u32[]{:S(2)}, u32[]{:S(2)}) async-start(bf16[1,128,3,32,128]{1,4,2,0,3:T(8,128)(2,1)} %copy.39), calls=%async_computation | async-start | bytes 6291456 | tf_op jit(solution)/shard_map/all_to_all | solution.py:78
  68.6 144.5 %all-to-all-done = bf16[1,128,3,32,128]{1,4,2,0,3:T(8,128)(2,1)} async-done(((bf16[1,128,3,32,128]{1,4,2,0,3:T(8,128)(2,1)}), bf16[1,128,3,32,128]{1,4,2,0,3:T(8,128)(2,1)}, u32[]{:S(2)}, u32[]{:S(2)}) %all-to-all-start) | async-done | bytes 3145760 | tf_op jit(solution)/shard_map/all_to_all | solution.py:78
  213.1 3.7 %copy.40 = bf16[1,128,3,32,128]{4,1,3,2,0:T(8,128)(2,1)S(1)} copy(bf16[1,128,3,32,128]{1,4,2,0,3:T(8,128)(2,1)} %all-to-all-done) | data formatting | bytes 6291456 | tf_op jit(solution)/shard_map/all_to_all | solution.py:78
  219.0 1.0 fusion.142
  220.0 1.1 fusion.143
  221.1 1.3 fusion.144
  222.4 1.5 fusion.145
  223.9 1.7 fusion.146
  227.2 0.8 fusion.98
  228.7 1.0 fusion.110
  229.7 0.8 fusion.6
  230.5 1.4 fusion.104
  231.9 1.0 fusion.4
  232.9 1.3 fusion.116
  234.2 1.1 fusion.2
  235.4 1.5 fusion.122
  236.9 1.3 fusion
  238.2 1.7 fusion.92
  239.9 1.0 copy-done
  240.9 5.0 %copy.41 = bf16[1,4096,1,128]{3,2,0,1:T(2,128)(2,1)S(1)} copy(bf16[1,4096,1,128]{1,3,2,0:T(8,128)(2,1)} %bitcast.263) | data formatting | bytes 2097152 | tf_op jit(solution)/shard_map/while/body/jit(dynamic_update_index_in_dim)/broadcast_in_dim | solution.py:77
  246.4 22.7 %reduce.32 = bf16[4096,128]{1,0:T(8,128)(2,1)S(1)} reduce(bf16[4096,1,1,128]{3,2,1,0:T(2,128)(2,1)S(1)} %bitcast.260, bf16[]{:T(256)} %broadcast.225), dimensions={1,2}, to_apply=%bitcast.207.reduce_sub_computation | reduce | bytes 2097154
  269.4 59.1 %all_to_all.30 = bf16[32,2,8192]{2,1,0:T(2,128)(2,1)S(1)} all-to-all(bf16[32,2,8192]{2,1,0:T(2,128)(2,1)S(1)} %reshape.392), channel_id=1, replica_groups=mesh['ctx'=32,'fsdp'=16] {'ctx'}, dimensions={0} | all-to-all | bytes 2097152 | tf_op jit(solution)/shard_map/all_to_all | solution.py:80
  328.4 1.0 reshape.393
  330.3 1.3 copy.43
  (26 shorter events, 6.3 us)
Async XLA Ops:
  3.5 9.7 %copy-start.1 = (f32[3,3,256]{2,1,0:T(4,128)S(1)}, f32[3,3,256]{2,1,0:T(4,128)}, u32[]{:S(2)}) copy-start(f32[3,3,256]{2,1,0:T(4,128)} %param.3) | copy-start | bytes 27652
  9.3 28.9 %collective-permute-start = (bf16[1,2,3,32,128]{4,3,2,1,0:T(8,128)(2,1)S(1)}, bf16[1,2,3,32,128]{4,3,2,1,0:T(8,128)(2,1)}, u32[]{:S(2)}, u32[]{:S(2)}) collective-permute-start(bf16[1,2,3,32,128]{4,3,2,1,0:T(8,128)(2,1)S(1)} %copy.36), channel_id=1, source_target_pairs={{0,16},{16,32},{32,48},{48,64},{64,80},{80,96},{96,112},{112,128},... | collective-permute-start | bytes 147464 | tf_op jit(solution)/shard_map/ppermute | solution.py:14
  54.0 159.2 %all-to-all-start = ((bf16[1,128,3,32,128]{1,4,2,0,3:T(8,128)(2,1)}), bf16[1,128,3,32,128]{1,4,2,0,3:T(8,128)(2,1)}, u32[]{:S(2)}, u32[]{:S(2)}) async-start(bf16[1,128,3,32,128]{1,4,2,0,3:T(8,128)(2,1)} %copy.39), calls=%async_computation | async-start | bytes 6291456 | tf_op jit(solution)/shard_map/all_to_all | solution.py:78
  239.9 1.0 copy-start
where the time goes:
time: 332 us
  waiting for transfers between devices  145 us (44%)
  blocking collectives  84 us (25%)
  other arithmetic  38.9 us (12%)
  local copies, waits for them, and re-layouts  28.7 us (9%)
  starting transfers between devices  18.4 us (6%)
  matrix products  16.8 us (5%)
    all_to_all x1, waiting for transfers between devices, on_device(): lax.all_to_all(outgoing, 'ctx', split_axis=3, concat_axis=1, tiled=True)  145 us
    all_to_all x1, blocking collectives, on_device(): lax.all_to_all(for_sending(per_head), 'ctx', split_axis=1, concat_axis=2,...  59.1 us
    all_gather x1, blocking collectives, on_device(): lax.all_gather(filters, 'fsdp', axis=2, tiled=True)  24.9 us
    unnamed x1, other arithmetic  22.7 us
    all_to_all x1, starting transfers between devices, on_device(): lax.all_to_all(outgoing, 'ctx', split_axis=3, concat_axis=1, tiled=True)  14.5 us
    convert_element_type x1, other arithmetic, featurize(): return summed.astype(jnp.bfloat16)  10 us
    dot_general x8, matrix products, attend_one(): jnp.einsum('hqk,khe->qhe', weights, values_all[:final], preferred_element...  8.6 us
    dot_general x8, matrix products, attend_one(): jnp.einsum('qhe,khe->hqk', queries[first:final], keys_all[:final], prefer...  8.23 us
  transfers between devices with their start and end apart: 2, of which 1 were waited for; matrix products, arithmetic and copies ran while one was open for 0% of the time, Pallas kernels for 0%

commit v1 on v0

v1 whole, which is shorter than its diff:
```python
import functools
import math

import jax
import jax.numpy as jnp
from jax import lax
from jax.experimental import pallas as pl
from jax.experimental.pallas import tpu as pltpu
from jax.sharding import PartitionSpec as P

HEADS = 32
HEAD_DIM = 128
TAPS = 3
SCALE = HEAD_DIM**-0.5 * math.log2(math.e)


def featurize_into(x_ref, column, taps_ref, stream, store):
    length = x_ref.shape[0]
    rows = 256
    taps = [taps_ref[stream, offset : offset + 1, :] for offset in range(TAPS)]

    def step(number, rim):
        first = pl.multiple_of(number * rows, rows)
        x = x_ref[pl.ds(first, rows), column : column + HEAD_DIM].astype(jnp.float32)
        extended = jnp.concatenate([rim, x], axis=0)
        summed = taps[0] * x + taps[1] * extended[7 : 7 + rows] + taps[2] * extended[6 : 6 + rows]
        store(first, rows, summed)
        return x[rows - 8 :]

    lax.fori_loop(0, length // rows, step, jnp.zeros((8, HEAD_DIM), jnp.float32))


def attention_kernel(bq, bk, x_ref, taps_ref, o_ref, qf, kf, vt, held, acc):
    length = x_ref.shape[0]

    def store_q(first, rows, summed):
        qf[pl.ds(first, rows), :] = summed.astype(jnp.bfloat16)

    def store_k(first, rows, summed):
        kf[pl.ds(first, rows), :] = summed.astype(jnp.bfloat16)

    def store_v(first, rows, summed):
        vt[:, pl.ds(first, rows)] = summed.T.astype(jnp.bfloat16)

    featurize_into(x_ref, 0, taps_ref, 0, store_q)
    featurize_into(x_ref, HEAD_DIM, taps_ref, 1, store_k)
    featurize_into(x_ref, 2 * HEAD_DIM, taps_ref, 2, store_v)

    def scores(q, j):
        k = kf[pl.ds(pl.multiple_of(j * bk, bk), bk), :]
        return lax.dot_general(k, q, (((1,), (1,)), ((), ())), preferred_element_type=jnp.float32)

    def process(s, j, m, l):
        new = jnp.maximum(m, jnp.max(s, axis=0, keepdims=True))
        alpha = jnp.exp2((m - new) * SCALE)
        p = jnp.exp2((s - new) * SCALE)
        l = l * alpha + jnp.sum(p, axis=0, keepdims=True)
        v = vt[:, pl.ds(pl.multiple_of(j * bk, bk), bk)]
        acc[...] = acc[...] * alpha + jnp.dot(
            v, p.astype(jnp.bfloat16), preferred_element_type=jnp.float32
        )
        return new, l

    def q_block(i, _):
        first = pl.multiple_of(i * bq, bq)
        q = qf[pl.ds(first, bq), :]
        acc[...] = jnp.zeros_like(acc)
        full = (i * bq) // bk
        held[0] = scores(q, 0)

        def body(j, ml):
            slot = lax.rem(j, 2)
            held[1 - slot] = scores(q, j + 1)
            return process(held[slot], j, *ml)

        start = (jnp.full((1, bq), -jnp.inf, jnp.float32), jnp.zeros((1, bq), jnp.float32))
        m, l = lax.fori_loop(0, full, body, start)
        key_pos = full * bk + lax.broadcasted_iota(jnp.int32, (bk, bq), 0)
        query_pos = i * bq + lax.broadcasted_iota(jnp.int32, (bk, bq), 1)
        s = jnp.where(key_pos <= query_pos, held[lax.rem(full, 2)], -jnp.inf)
        m, l = process(s, full, m, l)
        o_ref[pl.ds(first, bq), :] = (acc[...] / l).T.astype(jnp.bfloat16)
        return 0

    lax.fori_loop(0, length // bq, q_block, 0)


def attend(x, taps, bq=1024, bk=1024):
    length = x.shape[0]
    return pl.pallas_call(
        functools.partial(attention_kernel, bq, bk),
        out_shape=jax.ShapeDtypeStruct((length, HEAD_DIM), jnp.bfloat16),
        in_specs=[pl.BlockSpec(memory_space=pltpu.VMEM)] * 2,
        out_specs=pl.BlockSpec(memory_space=pltpu.VMEM),
        scratch_shapes=[
            pltpu.VMEM((length, HEAD_DIM), jnp.bfloat16),
            pltpu.VMEM((length, HEAD_DIM), jnp.bfloat16),
            pltpu.VMEM((HEAD_DIM, length), jnp.bfloat16),
            pltpu.VMEM((2, bk, bq), jnp.float32),
            pltpu.VMEM((HEAD_DIM, bq), jnp.float32),
        ],
        compiler_params=pltpu.CompilerParams(vmem_limit_bytes=44 * 2**20),
        name="attention",
    )(x, taps)


def own_taps(filters):
    head = lax.axis_index("ctx")
    here = filters.shape[2] // HEAD_DIM
    mine = lax.dynamic_slice_in_dim(filters, (head % here) * HEAD_DIM, HEAD_DIM, axis=2)
    mine = jnp.where(head // here == lax.axis_index("fsdp"), mine, 0.0)
    return lax.psum(mine, "fsdp")


def on_device(streams, filters):
    seqs_here, positions, channel_width = streams.shape
    taps = own_taps(filters)
    by_head = streams.reshape(positions, 3, HEADS, HEAD_DIM).transpose(2, 0, 1, 3)
    by_head = by_head.reshape(HEADS, positions, 3 * HEAD_DIM)
    arrived = lax.all_to_all(by_head, "ctx", split_axis=0, concat_axis=0, tiled=True)
    attended = attend(arrived.reshape(HEADS * positions, 3 * HEAD_DIM), taps)
    outgoing = attended.reshape(HEADS, positions, HEAD_DIM)
    returned = lax.all_to_all(outgoing, "ctx", split_axis=0, concat_axis=0, tiled=True)
    return returned.transpose(1, 0, 2).reshape(seqs_here, positions, HEADS * HEAD_DIM)


def solution(mesh):
    placed = (P("fsdp", "ctx", None), P(None, None, "fsdp"))
    return jax.shard_map(
        on_device, mesh=mesh, in_specs=placed, out_specs=P("fsdp", "ctx", None), check_vma=False
    )
```

time: 332 us -> 256 us (0.77)
  the two profiles are of different devices: /device:TPU:32 before, /device:TPU:56 now
where the time goes in v1:
time: 256 us; the launch traced here: 255 us
  waiting for transfers between devices  113 us (44%)
  blocking collectives  90 us (35%)
  Pallas kernels  25 us (10%)
  starting transfers between devices  16.5 us (6%)
  local copies, waits for them, and re-layouts  10.8 us (4%)
    all_to_all x1, waiting for transfers between devices, on_device(): lax.all_to_all(by_head, 'ctx', split_axis=0, concat_axis=0, tiled=True)  113 us
    all_to_all x1, blocking collectives, on_device(): lax.all_to_all(outgoing, 'ctx', split_axis=0, concat_axis=0, tiled=True)  59.5 us
    psum x1, blocking collectives, own_taps(): return lax.psum(mine, 'fsdp')  30.5 us
    pallas_call x1, Pallas kernels, attend(): pl.pallas_call(functools.partial(attention_kernel, bq, bk), out_shape=jax...  25 us
    all_to_all x1, starting transfers between devices, on_device(): lax.all_to_all(by_head, 'ctx', split_axis=0, concat_axis=0, tiled=True)  16.5 us
  transfers between devices with their start and end apart: 1, of which 1 were waited for; matrix products, arithmetic and copies ran while one was open for 0% of the time, Pallas kernels for 0%

profile of v1, /device:TPU:56, one launch (start us, length us, event | category | flops | bytes accessed | tf_op | source)
XLA Modules:
  0.0 255.4 jit_solution(17590331969301252655)
XLA Ops:
  0.0 3.5 %copy.7 = bf16[1,128,12288]{1,2,0:T(8,128)(2,1)S(1)} copy(bf16[1,128,12288]{2,1,0:T(8,128)(2,1)} %param.2) | data formatting | bytes 6291456 | tf_op args[0]
  3.5 1.9 copy.8
  5.4 0.0 copy-start
  5.4 16.5 %all-to-all-start = ((bf16[32,128,384]{1,2,0:T(8,128)(2,1)}), bf16[32,128,384]{1,2,0:T(8,128)(2,1)}, u32[]{:S(2)}, u32[]{:S(2)}) async-start(bf16[32,128,384]{1,2,0:T(8,128)(2,1)} %bitcast.2), calls=%async_computation | async-start | bytes 6291456 | tf_op jit(solution)/shard_map/all_to_all | solution.py:120
  21.9 0.0 copy-done
  21.9 30.5 %psum.7.taps_ref = f32[3,3,128]{2,1,0:T(4,128)S(1)} all-reduce(f32[3,3,128]{2,1,0:T(4,128)S(1)} %dynamic-slice_select_fusion), channel_id=1, replica_groups=mesh['ctx'=32,'fsdp'=16] {'fsdp'}, use_global_device_ids=true, to_apply=%region_0.1 | all-reduce | flops 1152 | bytes 9216 | tf_op jit(solution)/shard_map/psum | solution.py:112
  52.5 113.0 %all-to-all-done = bf16[32,128,384]{1,2,0:T(8,128)(2,1)} async-done(((bf16[32,128,384]{1,2,0:T(8,128)(2,1)}), bf16[32,128,384]{1,2,0:T(8,128)(2,1)}, u32[]{:S(2)}, u32[]{:S(2)}) %all-to-all-start) | async-done | bytes 3145760 | tf_op jit(solution)/shard_map/all_to_all | solution.py:120
  165.5 3.4 %copy.9 = bf16[32,128,384]{2,1,0:T(8,128)(2,1)S(1)} copy(bf16[32,128,384]{1,2,0:T(8,128)(2,1)} %all-to-all-done) | data formatting | bytes 6291456 | tf_op jit(solution)/shard_map/all_to_all | solution.py:120
  168.9 25.0 %attention.1 = bf16[4096,128]{1,0:T(8,128)(2,1)S(1)} custom-call(bf16[4096,384]{1,0:T(8,128)(2,1)S(1)} %bitcast.7, f32[3,3,128]{2,1,0:T(4,128)S(1)} %psum.7.taps_ref), custom_call_target="tpu_custom_call" | custom-call | tf_op jit(solution)/shard_map/attention/pallas_call | solution.py:90
  193.9 59.5 %all_to_all.10 = bf16[32,128,128]{2,1,0:T(8,128)(2,1)S(1)} all-to-all(bf16[32,128,128]{2,1,0:T(8,128)(2,1)S(1)} %bitcast.8), channel_id=1, replica_groups=mesh['ctx'=32,'fsdp'=16] {'ctx'}, dimensions={0} | all-to-all | bytes 2097152 | tf_op jit(solution)/shard_map/all_to_all | solution.py:123
  253.4 0.7 copy.10
  254.1 1.3 reshape.19
  (1 shorter events, 0.0 us)
Async XLA Ops:
  5.4 16.5 %copy-start = (f32[3,3,256]{2,1,0:T(4,128)S(1)}, f32[3,3,256]{2,1,0:T(4,128)}, u32[]{:S(2)}) copy-start(f32[3,3,256]{2,1,0:T(4,128)} %param.3) | copy-start | bytes 27652
  5.4 160.1 %all-to-all-start = ((bf16[32,128,384]{1,2,0:T(8,128)(2,1)}), bf16[32,128,384]{1,2,0:T(8,128)(2,1)}, u32[]{:S(2)}, u32[]{:S(2)}) async-start(bf16[32,128,384]{1,2,0:T(8,128)(2,1)} %bitcast.2), calls=%async_computation | async-start | bytes 6291456 | tf_op jit(solution)/shard_map/all_to_all | solution.py:120

commit v2 on v1

v2 whole, which is shorter than its diff:
```python
import functools
import math

import jax
import jax.numpy as jnp
from jax import lax
from jax.experimental import pallas as pl
from jax.experimental.pallas import tpu as pltpu
from jax.sharding import PartitionSpec as P

HEADS = 32
HEAD_DIM = 128
TAPS = 3
SCALE = HEAD_DIM**-0.5 * math.log2(math.e)
TILE = 256
STRETCH = 1024
ROWS = 16
HEADS_AT_A_TIME = 8
HEADROOM = 60.0
VMEM = pl.BlockSpec(memory_space=pltpu.VMEM)


def split_kernel(x_ref, out_ref, rows, by_head, arrived, sent):
    positions, width = x_ref.shape
    step = HEADS_AT_A_TIME * HEAD_DIM

    def fetch(part):
        columns = pl.ds(part * step, step)
        return pltpu.make_async_copy(x_ref.at[:, columns], rows.at[:, columns], arrived.at[part])

    def send(part):
        stream, first = divmod(part * HEADS_AT_A_TIME, HEADS)
        heads, kept = pl.ds(first, HEADS_AT_A_TIME), pl.ds(stream * positions, positions)
        place = out_ref.at[heads, kept, :]
        return pltpu.make_async_copy(by_head.at[heads, kept, :], place, sent.at[part])

    for part in range(width // step):
        fetch(part).start()
    for part in range(width // step):
        fetch(part).wait()
        for column in range(part * HEADS_AT_A_TIME, (part + 1) * HEADS_AT_A_TIME):
            stream, head = divmod(column, HEADS)
            by_head[head, stream * positions : (stream + 1) * positions, :] = rows[
                :, column * HEAD_DIM : (column + 1) * HEAD_DIM
            ]
        send(part).start()
    for part in range(width // step):
        send(part).wait()


def split_by_head(streams):
    positions, width = streams.shape
    parts = 3 * HEADS // HEADS_AT_A_TIME
    shape = (HEADS, 3 * positions, HEAD_DIM)
    return pl.pallas_call(
        split_kernel,
        out_shape=jax.ShapeDtypeStruct(shape, jnp.bfloat16),
        in_specs=[pl.BlockSpec(memory_space=pltpu.HBM)],
        out_specs=pl.BlockSpec(memory_space=pltpu.HBM),
        scratch_shapes=[
            pltpu.VMEM((positions, width), jnp.bfloat16),
            pltpu.VMEM(shape, jnp.bfloat16),
            pltpu.SemaphoreType.DMA((parts,)),
            pltpu.SemaphoreType.DMA((parts,)),
        ],
        compiler_params=pltpu.CompilerParams(vmem_limit_bytes=58 * 2**20),
        name="split_by_head",
    )(streams)


def merge_kernel(in_ref, out_ref, rows, sent):
    heads, positions, _ = in_ref.shape
    count = positions // ROWS

    def copy(part):
        chunk = pl.ds(part * ROWS, ROWS)
        return pltpu.make_async_copy(rows.at[chunk, :], out_ref.at[chunk, :], sent.at[part])

    for part in range(count):
        first = part * ROWS
        for head in range(heads):
            rows[first : first + ROWS, head * HEAD_DIM : (head + 1) * HEAD_DIM] = in_ref[
                head, first : first + ROWS, :
            ]
        copy(part).start()
    for part in range(count):
        copy(part).wait()


def merge_heads(parts):
    heads, positions, _ = parts.shape
    return pl.pallas_call(
        merge_kernel,
        out_shape=jax.ShapeDtypeStruct((positions, heads * HEAD_DIM), jnp.bfloat16),
        in_specs=[VMEM],
        out_specs=pl.BlockSpec(memory_space=pltpu.HBM),
        scratch_shapes=[
            pltpu.VMEM((positions, heads * HEAD_DIM), jnp.bfloat16),
            pltpu.SemaphoreType.DMA((positions // ROWS,)),
        ],
        compiler_params=pltpu.CompilerParams(vmem_limit_bytes=16 * 2**20),
        name="merge_heads",
    )(parts)


def sublanes(x):
    return x.reshape(x.shape[0] // 8, 8, x.shape[1])


def attention_kernel(x_ref, taps_ref, o_ref, qt, kf, vt, held, *weights):
    shards, positions = x_ref.shape[0], x_ref.shape[1] // 3
    length = shards * positions
    taps = [[taps_ref[s, offset : offset + 1, :] for offset in range(TAPS)] for s in range(3)]

    def featurize(first, rows):
        for s in range(3):
            shard, after = first // positions, (first + rows) // positions
            x = x_ref[shard:after, s * positions : (s + 1) * positions, :]
            x = x.reshape(rows, HEAD_DIM).astype(jnp.float32)
            held[s, 8 + first : 8 + first + rows] = x
            summed = taps[s][0] * x
            for offset in range(1, TAPS):
                start = 8 - offset + first
                summed = summed + taps[s][offset] * held[s, start : start + rows]
            featured = summed.astype(jnp.bfloat16)
            if s == 1:
                kf[first : first + rows, :] = featured
            else:
                (qt if s == 0 else vt)[:, first : first + rows] = featured.T

    def scores(key, q):
        return jnp.dot(kf[pl.ds(key, TILE), :], q, preferred_element_type=jnp.float32)

    down = lax.broadcasted_iota(jnp.int32, (TILE, TILE), 0)
    across = lax.broadcasted_iota(jnp.int32, (TILE, TILE), 1)

    def attend(t):
        first, end = t * TILE, (t + 1) * TILE
        rounded = weights[t % len(weights)]
        q = qt[:, first:end]
        s = sublanes(jnp.where(down <= across, scores(first, q), -jnp.inf))
        shift = jnp.max(s, axis=0)
        shift = jnp.broadcast_to(jnp.max(shift, axis=0, keepdims=True), shift.shape)
        exponent = jnp.exp2((s - shift) * SCALE)
        total, highest = jnp.sum(exponent, axis=0), shift
        rounded[first:end] = exponent.reshape(TILE, TILE).astype(jnp.bfloat16)
        for key in range(0, first, TILE):
            s = sublanes(scores(key, q))
            highest = jnp.maximum(highest, jnp.max(s, axis=0))
            exponent = jnp.exp2((s - shift) * SCALE)
            total = total + jnp.sum(exponent, axis=0)
            rounded[key : key + TILE] = exponent.reshape(TILE, TILE).astype(jnp.bfloat16)
        summed = jnp.dot(vt[:, :end], rounded[:end], preferred_element_type=jnp.float32)
        attended = summed / jnp.sum(total, axis=0, keepdims=True)
        o_ref[first:end, :] = attended.T.astype(jnp.bfloat16)
        return jnp.max(highest - shift)

    for s in range(3):
        held[s, :8] = jnp.zeros((8, HEAD_DIM), jnp.float32)
    above = 0.0
    for t in range(length // TILE):
        if (t * TILE) % STRETCH == 0:
            featurize(t * TILE, STRETCH)
        above = jnp.maximum(above, attend(t))

    @pl.when(above * SCALE > HEADROOM)
    def _():
        def query_tile(t, _):
            first = pl.multiple_of(t * TILE, TILE)
            q = qt[:, pl.ds(first, TILE)]

            def key_tile(number, carry):
                m, l, acc = carry
                key = pl.multiple_of(number * TILE, TILE)
                s = jnp.where(key + down <= first + across, scores(key, q), -jnp.inf)
                new = jnp.maximum(m, jnp.max(s, axis=0, keepdims=True))
                alpha = jnp.exp2((m - new) * SCALE)
                exponent = jnp.exp2((s - new) * SCALE)
                l = l * alpha + jnp.sum(exponent, axis=0, keepdims=True)
                acc = acc * alpha + jnp.dot(
                    vt[:, pl.ds(key, TILE)],
                    exponent.astype(jnp.bfloat16),
                    preferred_element_type=jnp.float32,
                )
                return new, l, acc

            start = (
                jnp.full((1, TILE), -jnp.inf, jnp.float32),
                jnp.zeros((1, TILE), jnp.float32),
                jnp.zeros((HEAD_DIM, TILE), jnp.float32),
            )
            _, l, acc = lax.fori_loop(0, t + 1, key_tile, start)
            o_ref[pl.ds(first, TILE), :] = (acc / l).T.astype(jnp.bfloat16)
            return 0

        lax.fori_loop(0, length // TILE, query_tile, 0)


def attention(x, taps):
    shards, rows, _ = x.shape
    length = shards * rows // 3
    return pl.pallas_call(
        attention_kernel,
        out_shape=jax.ShapeDtypeStruct((length, HEAD_DIM), jnp.bfloat16),
        in_specs=[VMEM] * 2,
        out_specs=VMEM,
        scratch_shapes=[
            pltpu.VMEM((HEAD_DIM, length), jnp.bfloat16),
            pltpu.VMEM((length, HEAD_DIM), jnp.bfloat16),
            pltpu.VMEM((HEAD_DIM, length), jnp.bfloat16),
            pltpu.VMEM((3, 8 + length, HEAD_DIM), jnp.float32),
            pltpu.VMEM((length, TILE), jnp.bfloat16),
            pltpu.VMEM((length, TILE), jnp.bfloat16),
        ],
        compiler_params=pltpu.CompilerParams(vmem_limit_bytes=32 * 2**20),
        name="attention",
    )(x, taps)


def own_taps(filters):
    head = lax.axis_index("ctx")
    here = filters.shape[2] // HEAD_DIM
    mine = lax.dynamic_slice_in_dim(filters, (head % here) * HEAD_DIM, HEAD_DIM, axis=2)
    mine = jnp.where(head // here == lax.axis_index("fsdp"), mine, 0.0)
    return lax.psum(mine, "fsdp")


def exchanged(parts):
    return lax.all_to_all(parts, "ctx", split_axis=0, concat_axis=0, tiled=True)


def on_device(streams, filters):
    seqs_here, positions, channel_width = streams.shape
    taps = own_taps(filters)
    arrived = exchanged(split_by_head(streams.reshape(positions, channel_width)))
    attended = attention(arrived, taps)
    returned = exchanged(attended.reshape(HEADS, positions, HEAD_DIM))
    return merge_heads(returned).reshape(seqs_here, positions, HEADS * HEAD_DIM)


def solution(mesh):
    placed = (P("fsdp", "ctx", None), P(None, None, "fsdp"))
    return jax.shard_map(
        on_device, mesh=mesh, in_specs=placed, out_specs=P("fsdp", "ctx", None), check_vma=False
    )
```

time: 256 us -> 294 us (1.15)
  Pallas kernels: 25 us -> 74.2 us
  local copies, waits for them, and re-layouts: 10.8 us -> 0.01 us
    pallas_call x1 -> x3, Pallas kernels: 25 us -> 74.2 us  [the longest x1 70.3 us: attention(): pl.pallas_call(attention_kernel, out_shape=jax.ShapeDtypeStruct((length,...]
    unnamed x3 -> x2, local copies, waits for them, and re-layouts: 3.48 us -> 0.01 us
    all_to_all x1 -> x0, local copies, waits for them, and re-layouts: 3.41 us -> none  [on_device(): lax.all_to_all(by_head, 'ctx', split_axis=0, concat_axis=0, tiled=True)]
where the time goes in v2:
time: 294 us
  waiting for transfers between devices  113 us (38%)
  blocking collectives  89.9 us (31%)
  Pallas kernels  74.2 us (25%)
  starting transfers between devices  16.3 us (6%)
    all_to_all x1, waiting for transfers between devices, exchanged(): return lax.all_to_all(parts, 'ctx', split_axis=0, concat_axis=0, tiled=True)  113 us
    pallas_call x1, Pallas kernels, attention(): pl.pallas_call(attention_kernel, out_shape=jax.ShapeDtypeStruct((length,...  70.3 us
    all_to_all x1, blocking collectives, exchanged(): return lax.all_to_all(parts, 'ctx', split_axis=0, concat_axis=0, tiled=True)  59.5 us
    psum x1, blocking collectives, own_taps(): return lax.psum(mine, 'fsdp')  30.3 us
    all_to_all x1, starting transfers between devices, exchanged(): return lax.all_to_all(parts, 'ctx', split_axis=0, concat_axis=0, tiled=True)  16.3 us
  transfers between devices with their start and end apart: 1, of which 1 were waited for; matrix products, arithmetic and copies ran while one was open for 0% of the time, Pallas kernels for 0%

profile of v2, /device:TPU:56, one launch (start us, length us, event | category | flops | bytes accessed | tf_op | source)
XLA Modules:
  0.0 293.6 jit_solution(11842934657710908410)
XLA Ops:
  0.0 2.9 split_by_head.1
  2.9 0.0 copy-start
  2.9 16.3 %all-to-all-start = ((bf16[32,384,128]{2,1,0:T(8,128)(2,1)}), bf16[32,384,128]{2,1,0:T(8,128)(2,1)S(1)}, u32[]{:S(2)}, u32[]{:S(2)}) async-start(bf16[32,384,128]{2,1,0:T(8,128)(2,1)} %split_by_head.1), calls=%async_computation | async-start | bytes 6291456 | tf_op jit(solution)/shard_map/all_to_all | solution.py:229
  19.2 0.0 copy-done
  19.3 30.3 %psum.7.taps_ref = f32[3,3,128]{2,1,0:T(4,128)S(1)} all-reduce(f32[3,3,128]{2,1,0:T(4,128)S(1)} %dynamic-slice_select_fusion), channel_id=1, replica_groups=mesh['ctx'=32,'fsdp'=16] {'fsdp'}, use_global_device_ids=true, to_apply=%region_0.1 | all-reduce | flops 1152 | bytes 9216 | tf_op jit(solution)/shard_map/psum | solution.py:225
  49.6 113.2 %all-to-all-done.x_ref = bf16[32,384,128]{2,1,0:T(8,128)(2,1)S(1)} async-done(((bf16[32,384,128]{2,1,0:T(8,128)(2,1)}), bf16[32,384,128]{2,1,0:T(8,128)(2,1)S(1)}, u32[]{:S(2)}, u32[]{:S(2)}) %all-to-all-start) | async-done | bytes 3145760 | tf_op jit(solution)/shard_map/all_to_all | solution.py:229
  162.8 70.3 %attention.1 = bf16[4096,128]{1,0:T(8,128)(2,1)S(1)} custom-call(bf16[32,384,128]{2,1,0:T(8,128)(2,1)S(1)} %all-to-all-done.x_ref, f32[3,3,128]{2,1,0:T(4,128)S(1)} %psum.7.taps_ref), custom_call_target="tpu_custom_call" | custom-call | tf_op jit(solution)/shard_map/attention/pallas_call | solution.py:202
  233.0 59.5 %all_to_all.10.in_ref = bf16[32,128,128]{2,1,0:T(8,128)(2,1)S(1)} all-to-all(bf16[32,128,128]{2,1,0:T(8,128)(2,1)S(1)} %bitcast.3), channel_id=1, replica_groups=mesh['ctx'=32,'fsdp'=16] {'ctx'}, dimensions={0} | all-to-all | bytes 2097152 | tf_op jit(solution)/shard_map/all_to_all | solution.py:229
  292.6 1.0 merge_heads.1
  (1 shorter events, 0.0 us)
Async XLA Ops:
  2.9 16.3 %copy-start = (f32[3,3,256]{2,1,0:T(4,128)S(1)}, f32[3,3,256]{2,1,0:T(4,128)}, u32[]{:S(2)}) copy-start(f32[3,3,256]{2,1,0:T(4,128)} %param.3) | copy-start | bytes 27652
  2.9 159.9 %all-to-all-start = ((bf16[32,384,128]{2,1,0:T(8,128)(2,1)}), bf16[32,384,128]{2,1,0:T(8,128)(2,1)S(1)}, u32[]{:S(2)}, u32[]{:S(2)}) async-start(bf16[32,384,128]{2,1,0:T(8,128)(2,1)} %split_by_head.1), calls=%async_computation | async-start | bytes 6291456 | tf_op jit(solution)/shard_map/all_to_all | solution.py:229

commit v3 on v2

--- a/solution.py
+++ b/solution.py
@@ -16,7 +16,7 @@
 STRETCH = 1024
 ROWS = 16
 HEADS_AT_A_TIME = 8
-HEADROOM = 60.0
+HIGHEST_TOTAL = 2.0**60
 VMEM = pl.BlockSpec(memory_space=pltpu.VMEM)
 
 
@@ -142,28 +142,27 @@
         shift = jnp.max(s, axis=0)
         shift = jnp.broadcast_to(jnp.max(shift, axis=0, keepdims=True), shift.shape)
         exponent = jnp.exp2((s - shift) * SCALE)
-        total, highest = jnp.sum(exponent, axis=0), shift
+        total = jnp.sum(exponent, axis=0)
         rounded[first:end] = exponent.reshape(TILE, TILE).astype(jnp.bfloat16)
         for key in range(0, first, TILE):
             s = sublanes(scores(key, q))
-            highest = jnp.maximum(highest, jnp.max(s, axis=0))
             exponent = jnp.exp2((s - shift) * SCALE)
             total = total + jnp.sum(exponent, axis=0)
             rounded[key : key + TILE] = exponent.reshape(TILE, TILE).astype(jnp.bfloat16)
         summed = jnp.dot(vt[:, :end], rounded[:end], preferred_element_type=jnp.float32)
-        attended = summed / jnp.sum(total, axis=0, keepdims=True)
-        o_ref[first:end, :] = attended.T.astype(jnp.bfloat16)
-        return jnp.max(highest - shift)
+        total = jnp.sum(total, axis=0, keepdims=True)
+        o_ref[first:end, :] = (summed / total).T.astype(jnp.bfloat16)
+        return jnp.max(total)
 
     for s in range(3):
         held[s, :8] = jnp.zeros((8, HEAD_DIM), jnp.float32)
-    above = 0.0
+    largest = 0.0
+    for first in range(0, length, STRETCH):
+        featurize(first, STRETCH)
     for t in range(length // TILE):
-        if (t * TILE) % STRETCH == 0:
-            featurize(t * TILE, STRETCH)
-        above = jnp.maximum(above, attend(t))
-
-    @pl.when(above * SCALE > HEADROOM)
+        largest = jnp.maximum(largest, attend(t))
+
+    @pl.when(jnp.logical_not(largest < HIGHEST_TOTAL))
     def _():
         def query_tile(t, _):
             first = pl.multiple_of(t * TILE, TILE)

time: 294 us -> 293 us (level)
  the two profiles are of different devices: /device:TPU:56 before, /device:TPU:48 now
where the time goes in v3:
time: 293 us
  waiting for transfers between devices  116 us (40%)
  blocking collectives  87.1 us (30%)
  Pallas kernels  73.4 us (25%)
  starting transfers between devices  16.3 us (6%)
    all_to_all x1, waiting for transfers between devices, exchanged(): return lax.all_to_all(parts, 'ctx', split_axis=0, concat_axis=0, tiled=True)  116 us
    pallas_call x1, Pallas kernels, attention(): pl.pallas_call(attention_kernel, out_shape=jax.ShapeDtypeStruct((length,...  69.5 us
    all_to_all x1, blocking collectives, exchanged(): return lax.all_to_all(parts, 'ctx', split_axis=0, concat_axis=0, tiled=True)  59.5 us
    psum x1, blocking collectives, own_taps(): return lax.psum(mine, 'fsdp')  27.6 us
    all_to_all x1, starting transfers between devices, exchanged(): return lax.all_to_all(parts, 'ctx', split_axis=0, concat_axis=0, tiled=True)  16.3 us
  transfers between devices with their start and end apart: 1, of which 1 were waited for; matrix products, arithmetic and copies ran while one was open for 0% of the time, Pallas kernels for 0%

profile of v3, /device:TPU:48, one launch (start us, length us, event | category | flops | bytes accessed | tf_op | source)
XLA Modules:
  0.0 292.8 jit_solution(18062222824644558776)
XLA Ops:
  0.0 2.9 split_by_head.1
  2.9 0.0 copy-start
  2.9 16.3 %all-to-all-start = ((bf16[32,384,128]{2,1,0:T(8,128)(2,1)}), bf16[32,384,128]{2,1,0:T(8,128)(2,1)S(1)}, u32[]{:S(2)}, u32[]{:S(2)}) async-start(bf16[32,384,128]{2,1,0:T(8,128)(2,1)} %split_by_head.1), calls=%async_computation | async-start | bytes 6291456 | tf_op jit(solution)/shard_map/all_to_all | solution.py:228
  19.2 0.0 copy-done
  19.3 27.6 %psum.7.taps_ref = f32[3,3,128]{2,1,0:T(4,128)S(1)} all-reduce(f32[3,3,128]{2,1,0:T(4,128)S(1)} %dynamic-slice_select_fusion), channel_id=1, replica_groups=mesh['ctx'=32,'fsdp'=16] {'fsdp'}, use_global_device_ids=true, to_apply=%region_0.1 | all-reduce | flops 1152 | bytes 9216 | tf_op jit(solution)/shard_map/psum | solution.py:224
  46.9 115.9 %all-to-all-done.x_ref = bf16[32,384,128]{2,1,0:T(8,128)(2,1)S(1)} async-done(((bf16[32,384,128]{2,1,0:T(8,128)(2,1)}), bf16[32,384,128]{2,1,0:T(8,128)(2,1)S(1)}, u32[]{:S(2)}, u32[]{:S(2)}) %all-to-all-start) | async-done | bytes 3145760 | tf_op jit(solution)/shard_map/all_to_all | solution.py:228
  162.8 69.5 %attention.1 = bf16[4096,128]{1,0:T(8,128)(2,1)S(1)} custom-call(bf16[32,384,128]{2,1,0:T(8,128)(2,1)S(1)} %all-to-all-done.x_ref, f32[3,3,128]{2,1,0:T(4,128)S(1)} %psum.7.taps_ref), custom_call_target="tpu_custom_call" | custom-call | tf_op jit(solution)/shard_map/attention/pallas_call | solution.py:201
  232.2 59.5 %all_to_all.10.in_ref = bf16[32,128,128]{2,1,0:T(8,128)(2,1)S(1)} all-to-all(bf16[32,128,128]{2,1,0:T(8,128)(2,1)S(1)} %bitcast.3), channel_id=1, replica_groups=mesh['ctx'=32,'fsdp'=16] {'ctx'}, dimensions={0} | all-to-all | bytes 2097152 | tf_op jit(solution)/shard_map/all_to_all | solution.py:228
  291.7 1.0 merge_heads.1
  (1 shorter events, 0.0 us)
Async XLA Ops:
  2.9 16.3 %copy-start = (f32[3,3,256]{2,1,0:T(4,128)S(1)}, f32[3,3,256]{2,1,0:T(4,128)}, u32[]{:S(2)}) copy-start(f32[3,3,256]{2,1,0:T(4,128)} %param.3) | copy-start | bytes 27652
  2.9 159.9 %all-to-all-start = ((bf16[32,384,128]{2,1,0:T(8,128)(2,1)}), bf16[32,384,128]{2,1,0:T(8,128)(2,1)S(1)}, u32[]{:S(2)}, u32[]{:S(2)}) async-start(bf16[32,384,128]{2,1,0:T(8,128)(2,1)} %split_by_head.1), calls=%async_computation | async-start | bytes 6291456 | tf_op jit(solution)/shard_map/all_to_all | solution.py:228

commit v4 on v3

--- a/solution.py
+++ b/solution.py
@@ -13,6 +13,7 @@
 TAPS = 3
 SCALE = HEAD_DIM**-0.5 * math.log2(math.e)
 TILE = 256
+HALF = TILE // 2
 STRETCH = 1024
 ROWS = 16
 HEADS_AT_A_TIME = 8
@@ -128,22 +129,33 @@
             else:
                 (qt if s == 0 else vt)[:, first : first + rows] = featured.T
 
-    def scores(key, q):
-        return jnp.dot(kf[pl.ds(key, TILE), :], q, preferred_element_type=jnp.float32)
+    def scores(key, q, count=TILE):
+        return jnp.dot(kf[pl.ds(key, count), :], q, preferred_element_type=jnp.float32)
 
     down = lax.broadcasted_iota(jnp.int32, (TILE, TILE), 0)
     across = lax.broadcasted_iota(jnp.int32, (TILE, TILE), 1)
+    causal = down <= across
 
     def attend(t):
         first, end = t * TILE, (t + 1) * TILE
         rounded = weights[t % len(weights)]
         q = qt[:, first:end]
-        s = sublanes(jnp.where(down <= across, scores(first, q), -jnp.inf))
-        shift = jnp.max(s, axis=0)
+        early = sublanes(jnp.where(causal[:HALF], scores(first, q, HALF), -jnp.inf))
+        late = scores(first + HALF, q[:, HALF:], HALF)
+        late = sublanes(jnp.where(causal[:HALF, :HALF], late, -jnp.inf))
+        shift = jnp.max(early, axis=0)
+        raised = jnp.maximum(shift[:, HALF:], jnp.max(late, axis=0))
+        shift = jnp.concatenate([shift[:, :HALF], raised], axis=1)
         shift = jnp.broadcast_to(jnp.max(shift, axis=0, keepdims=True), shift.shape)
-        exponent = jnp.exp2((s - shift) * SCALE)
-        total = jnp.sum(exponent, axis=0)
-        rounded[first:end] = exponent.reshape(TILE, TILE).astype(jnp.bfloat16)
+        early = jnp.exp2((early - shift) * SCALE)
+        late = jnp.exp2((late - shift[:, HALF:]) * SCALE)
+        total = jnp.sum(early, axis=0)
+        raised = total[:, HALF:] + jnp.sum(late, axis=0)
+        total = jnp.concatenate([total[:, :HALF], raised], axis=1)
+        middle = first + HALF
+        rounded[first:middle] = early.reshape(HALF, TILE).astype(jnp.bfloat16)
+        rounded[middle:end, :HALF] = jnp.zeros((HALF, HALF), jnp.bfloat16)
+        rounded[middle:end, HALF:] = late.reshape(HALF, HALF).astype(jnp.bfloat16)
         for key in range(0, first, TILE):
             s = sublanes(scores(key, q))
             exponent = jnp.exp2((s - shift) * SCALE)

time: 293 us -> 293 us (level)
  the two profiles are of different devices: /device:TPU:48 before, /device:TPU:56 now
where the time goes in v4:
time: 293 us
  waiting for transfers between devices  113 us (39%)
  blocking collectives  89.9 us (31%)
  Pallas kernels  73.3 us (25%)
  starting transfers between devices  16.3 us (6%)
    all_to_all x1, waiting for transfers between devices, exchanged(): return lax.all_to_all(parts, 'ctx', split_axis=0, concat_axis=0, tiled=True)  113 us
    pallas_call x1, Pallas kernels, attention(): pl.pallas_call(attention_kernel, out_shape=jax.ShapeDtypeStruct((length,...  69.3 us
    all_to_all x1, blocking collectives, exchanged(): return lax.all_to_all(parts, 'ctx', split_axis=0, concat_axis=0, tiled=True)  59.5 us
    psum x1, blocking collectives, own_taps(): return lax.psum(mine, 'fsdp')  30.3 us
    all_to_all x1, starting transfers between devices, exchanged(): return lax.all_to_all(parts, 'ctx', split_axis=0, concat_axis=0, tiled=True)  16.3 us
  transfers between devices with their start and end apart: 1, of which 1 were waited for; matrix products, arithmetic and copies ran while one was open for 0% of the time, Pallas kernels for 0%

profile of v4, /device:TPU:56, one launch (start us, length us, event | category | flops | bytes accessed | tf_op | source)
XLA Modules:
  0.0 292.7 jit_solution(953663718648715350)
XLA Ops:
  0.0 2.9 split_by_head.1
  2.9 0.0 copy-start
  2.9 16.3 %all-to-all-start = ((bf16[32,384,128]{2,1,0:T(8,128)(2,1)}), bf16[32,384,128]{2,1,0:T(8,128)(2,1)S(1)}, u32[]{:S(2)}, u32[]{:S(2)}) async-start(bf16[32,384,128]{2,1,0:T(8,128)(2,1)} %split_by_head.1), calls=%async_computation | async-start | bytes 6291456 | tf_op jit(solution)/shard_map/all_to_all | solution.py:240
  19.2 0.0 copy-done
  19.3 30.3 %psum.7.taps_ref = f32[3,3,128]{2,1,0:T(4,128)S(1)} all-reduce(f32[3,3,128]{2,1,0:T(4,128)S(1)} %dynamic-slice_select_fusion), channel_id=1, replica_groups=mesh['ctx'=32,'fsdp'=16] {'fsdp'}, use_global_device_ids=true, to_apply=%region_0.1 | all-reduce | flops 1152 | bytes 9216 | tf_op jit(solution)/shard_map/psum | solution.py:236
  49.6 113.2 %all-to-all-done.x_ref = bf16[32,384,128]{2,1,0:T(8,128)(2,1)S(1)} async-done(((bf16[32,384,128]{2,1,0:T(8,128)(2,1)}), bf16[32,384,128]{2,1,0:T(8,128)(2,1)S(1)}, u32[]{:S(2)}, u32[]{:S(2)}) %all-to-all-start) | async-done | bytes 3145760 | tf_op jit(solution)/shard_map/all_to_all | solution.py:240
  162.8 69.3 %attention.1 = bf16[4096,128]{1,0:T(8,128)(2,1)S(1)} custom-call(bf16[32,384,128]{2,1,0:T(8,128)(2,1)S(1)} %all-to-all-done.x_ref, f32[3,3,128]{2,1,0:T(4,128)S(1)} %psum.7.taps_ref), custom_call_target="tpu_custom_call" | custom-call | tf_op jit(solution)/shard_map/attention/pallas_call | solution.py:213
  232.1 59.5 %all_to_all.10.in_ref = bf16[32,128,128]{2,1,0:T(8,128)(2,1)S(1)} all-to-all(bf16[32,128,128]{2,1,0:T(8,128)(2,1)S(1)} %bitcast.3), channel_id=1, replica_groups=mesh['ctx'=32,'fsdp'=16] {'ctx'}, dimensions={0} | all-to-all | bytes 2097152 | tf_op jit(solution)/shard_map/all_to_all | solution.py:240
  291.6 1.0 merge_heads.1
  (1 shorter events, 0.0 us)
Async XLA Ops:
  2.9 16.3 %copy-start = (f32[3,3,256]{2,1,0:T(4,128)S(1)}, f32[3,3,256]{2,1,0:T(4,128)}, u32[]{:S(2)}) copy-start(f32[3,3,256]{2,1,0:T(4,128)} %param.3) | copy-start | bytes 27652
  2.9 159.9 %all-to-all-start = ((bf16[32,384,128]{2,1,0:T(8,128)(2,1)}), bf16[32,384,128]{2,1,0:T(8,128)(2,1)S(1)}, u32[]{:S(2)}, u32[]{:S(2)}) async-start(bf16[32,384,128]{2,1,0:T(8,128)(2,1)} %split_by_head.1), calls=%async_computation | async-start | bytes 6291456 | tf_op jit(solution)/shard_map/all_to_all | solution.py:240

commit v5 on v4

--- a/solution.py
+++ b/solution.py
@@ -171,7 +171,7 @@
     largest = 0.0
     for first in range(0, length, STRETCH):
         featurize(first, STRETCH)
-    for t in range(length // TILE):
+    for t in reversed(range(length // TILE)):
         largest = jnp.maximum(largest, attend(t))
 
     @pl.when(jnp.logical_not(largest < HIGHEST_TOTAL))

time: 293 us -> 293 us (level)
  the two profiles are of different devices: /device:TPU:56 before, /device:TPU:40 now
where the time goes in v5:
time: 293 us
  waiting for transfers between devices  110 us (38%)
  blocking collectives  92.9 us (32%)
  Pallas kernels  73.1 us (25%)
  starting transfers between devices  16.3 us (6%)
    all_to_all x1, waiting for transfers between devices, exchanged(): return lax.all_to_all(parts, 'ctx', split_axis=0, concat_axis=0, tiled=True)  110 us
    pallas_call x1, Pallas kernels, attention(): pl.pallas_call(attention_kernel, out_shape=jax.ShapeDtypeStruct((length,...  69.2 us
    all_to_all x1, blocking collectives, exchanged(): return lax.all_to_all(parts, 'ctx', split_axis=0, concat_axis=0, tiled=True)  59.5 us
    psum x1, blocking collectives, own_taps(): return lax.psum(mine, 'fsdp')  33.4 us
    all_to_all x1, starting transfers between devices, exchanged(): return lax.all_to_all(parts, 'ctx', split_axis=0, concat_axis=0, tiled=True)  16.3 us
  transfers between devices with their start and end apart: 1, of which 1 were waited for; matrix products, arithmetic and copies ran while one was open for 0% of the time, Pallas kernels for 0%

profile of v5, /device:TPU:40, one launch (start us, length us, event | category | flops | bytes accessed | tf_op | source)
XLA Modules:
  0.0 292.5 jit_solution(17539240321532817197)
XLA Ops:
  0.0 2.9 split_by_head.1
  2.9 0.0 copy-start
  2.9 16.3 %all-to-all-start = ((bf16[32,384,128]{2,1,0:T(8,128)(2,1)}), bf16[32,384,128]{2,1,0:T(8,128)(2,1)S(1)}, u32[]{:S(2)}, u32[]{:S(2)}) async-start(bf16[32,384,128]{2,1,0:T(8,128)(2,1)} %split_by_head.1), calls=%async_computation | async-start | bytes 6291456 | tf_op jit(solution)/shard_map/all_to_all | solution.py:240
  19.2 0.0 copy-done
  19.3 33.4 %psum.7.taps_ref = f32[3,3,128]{2,1,0:T(4,128)S(1)} all-reduce(f32[3,3,128]{2,1,0:T(4,128)S(1)} %dynamic-slice_select_fusion), channel_id=1, replica_groups=mesh['ctx'=32,'fsdp'=16] {'fsdp'}, use_global_device_ids=true, to_apply=%region_0.1 | all-reduce | flops 1152 | bytes 9216 | tf_op jit(solution)/shard_map/psum | solution.py:236
  52.7 110.1 %all-to-all-done.x_ref = bf16[32,384,128]{2,1,0:T(8,128)(2,1)S(1)} async-done(((bf16[32,384,128]{2,1,0:T(8,128)(2,1)}), bf16[32,384,128]{2,1,0:T(8,128)(2,1)S(1)}, u32[]{:S(2)}, u32[]{:S(2)}) %all-to-all-start) | async-done | bytes 3145760 | tf_op jit(solution)/shard_map/all_to_all | solution.py:240
  162.8 69.2 %attention.1 = bf16[4096,128]{1,0:T(8,128)(2,1)S(1)} custom-call(bf16[32,384,128]{2,1,0:T(8,128)(2,1)S(1)} %all-to-all-done.x_ref, f32[3,3,128]{2,1,0:T(4,128)S(1)} %psum.7.taps_ref), custom_call_target="tpu_custom_call" | custom-call | tf_op jit(solution)/shard_map/attention/pallas_call | solution.py:213
  232.0 59.5 %all_to_all.10.in_ref = bf16[32,128,128]{2,1,0:T(8,128)(2,1)S(1)} all-to-all(bf16[32,128,128]{2,1,0:T(8,128)(2,1)S(1)} %bitcast.3), channel_id=1, replica_groups=mesh['ctx'=32,'fsdp'=16] {'ctx'}, dimensions={0} | all-to-all | bytes 2097152 | tf_op jit(solution)/shard_map/all_to_all | solution.py:240
  291.5 1.0 merge_heads.1
  (1 shorter events, 0.0 us)
Async XLA Ops:
  2.9 16.3 %copy-start = (f32[3,3,256]{2,1,0:T(4,128)S(1)}, f32[3,3,256]{2,1,0:T(4,128)}, u32[]{:S(2)}) copy-start(f32[3,3,256]{2,1,0:T(4,128)} %param.3) | copy-start | bytes 27652
  2.9 159.9 %all-to-all-start = ((bf16[32,384,128]{2,1,0:T(8,128)(2,1)}), bf16[32,384,128]{2,1,0:T(8,128)(2,1)S(1)}, u32[]{:S(2)}, u32[]{:S(2)}) async-start(bf16[32,384,128]{2,1,0:T(8,128)(2,1)} %split_by_head.1), calls=%async_computation | async-start | bytes 6291456 | tf_op jit(solution)/shard_map/all_to_all | solution.py:240
